TPU v7x, 256 devices: a whole 4x4x8 slice. The times are simulated.
256 devices in a mesh: blk: 32 (over z, y_hi, core), rep: 8 (over y_lo, x).
Axes of the slice: x: 4, y: 4 (y_hi: 2, y_lo: 2; y = y_hi * 2 + y_lo), z: 8, core: 2. Of those that a mesh axis runs over, the one named last changes fastest.
Arguments:
- features: bfloat16 [65536, 128], P(('blk', 'rep')), may hold values from -6 to 6
- adj_tiles: bfloat16 [32, 8, 32, 8, 128, 128], P('blk', 'rep'), may hold values from -0.0625 to 0.0625
- tile_counts: int32 [32, 8, 32], P('blk', 'rep'), may hold values from 1 to 8
- dst_tile: int32 [32, 8, 32, 8], P('blk', 'rep'), may hold values from 0 to 15
- src_tile: int32 [32, 8, 32, 8], P('blk', 'rep'), may hold values from 0 to 1
- weight: float32 [128, 128], replicated, may hold values from -0.5 to 0.5
- bias_term: float32 [128], replicated, may hold values from -3 to 3
- cotangent: float32 [65536, 128], P(('blk', 'rep')), may hold values from -6 to 6
Outputs:
- activations: float32 [65536, 128], P(('blk', 'rep'))
- feature_grad: float32 [65536, 128], P(('blk', 'rep'))
- weight_grad: float32 [128, 128], replicated
All inputs are finite; a program needn't handle non-finite values.
Results may differ from a plain program's by a relative error of at most 0.0029.
Values may be sent and summed in bfloat16 or wider, within the bound.
A program may use at most 64 MiB of HBM per device.

v0:
```python
import math

import jax
import jax.numpy as jnp
from jax import lax
from jax.sharding import PartitionSpec as P


def passed_along(array, axis, by):
    devices = lax.axis_size(axis)
    return lax.ppermute(array, axis, [(i, (i + by) % devices) for i in range(devices)])


def body(features, adj_tiles, tile_counts, dst_tile, src_tile, weight, bias_term, cotangent):
    blocks = lax.axis_size("blk")
    group_size = lax.axis_size("rep")
    capacity = adj_tiles.shape[3]
    tile_len = adj_tiles.shape[4]
    own_rows, feature_len = features.shape
    shard_tiles = own_rows // tile_len
    block_tiles = shard_tiles * group_size
    own_tiles = adj_tiles[0, 0]
    counts = tile_counts[0, 0]
    dst_ids = dst_tile[0, 0]
    src_ids = src_tile[0, 0]
    slot_ids = jnp.arange(capacity)

    def live_of(s):
        return (slot_ids < counts[s]).astype(jnp.float32)

    def forward_term(s, visiting, partial_value):
        picked = jnp.take(visiting, src_ids[s], axis=0)
        product = jnp.einsum(
            "ktu,kuf->ktf", own_tiles[s], picked, preferred_element_type=jnp.float32
        )
        placing = (jnp.arange(block_tiles)[:, None] == dst_ids[s][None, :]).astype(
            jnp.float32
        ) * live_of(s)[None, :]
        return partial_value + jnp.dot(
            placing, product.reshape(capacity, -1), precision=lax.Precision.HIGHEST
        )

    visiting = features.reshape(shard_tiles, tile_len, feature_len)
    partial_value = jnp.zeros((block_tiles, tile_len * feature_len), jnp.float32)
    partial_value = forward_term(0, visiting, partial_value)

    def cycle_turn(s, loop_state):
        moving, summed = loop_state
        moving = passed_along(moving, "blk", 1)
        return (moving, forward_term(s, moving, summed))

    moving, partial_value = lax.fori_loop(1, blocks, cycle_turn, (visiting, partial_value))
    aggregate = lax.psum_scatter(
        partial_value.reshape(block_tiles * tile_len, feature_len),
        "rep",
        scatter_dimension=0,
        tiled=True,
    )
    pre_act = jnp.dot(aggregate, weight, precision=lax.Precision.HIGHEST) + bias_term
    activations = jax.nn.silu(pre_act)
    sigmoid_val = jax.nn.sigmoid(pre_act)
    pre_grad = cotangent * sigmoid_val * (1.0 + pre_act * (1.0 - sigmoid_val))
    node_total = own_rows * blocks * group_size
    weight_term = jnp.dot(aggregate.T, pre_grad, precision=lax.Precision.HIGHEST)
    weight_grad = lax.psum(weight_term, ("blk", "rep")) / math.sqrt(node_total)
    agg_grad = jnp.dot(pre_grad, weight.T, precision=lax.Precision.HIGHEST).astype(jnp.bfloat16)
    block_grad = lax.all_gather(agg_grad, "rep", axis=0, tiled=True).reshape(
        block_tiles, tile_len, feature_len
    )

    def backward_term(s):
        rows_sel = jnp.take(block_grad, dst_ids[s], axis=0)
        product = jnp.einsum(
            "ktu,ktf->kuf", own_tiles[s], rows_sel, preferred_element_type=jnp.float32
        )
        placing = (jnp.arange(shard_tiles)[:, None] == src_ids[s][None, :]).astype(
            jnp.float32
        ) * live_of(s)[None, :]
        return jnp.dot(placing, product.reshape(capacity, -1), precision=lax.Precision.HIGHEST)

    def grad_turn(t, carried):
        carried = passed_along(carried, "blk", 1)
        return carried + backward_term((t + 1) % blocks)

    carried = lax.fori_loop(1, blocks, grad_turn, backward_term(1 % blocks))
    feature_grad = carried.reshape(own_rows, feature_len)
    return (activations, feature_grad, weight_grad)


def solution(mesh):
    in_specs = (
        P(("blk", "rep"), None),
        P("blk", "rep", None, None, None, None),
        P("blk", "rep", None),
        P("blk", "rep", None, None),
        P("blk", "rep", None, None),
        P(),
        P(),
        P(("blk", "rep"), None),
    )
    out_specs = (P(("blk", "rep"), None), P(("blk", "rep"), None), P())
    return jax.shard_map(body, mesh=mesh, in_specs=in_specs, out_specs=out_specs, check_vma=False)
```

profile of v0, /device:TPU:1, one launch (start us, length us, event | category | flops | bytes accessed | tf_op | source)
XLA Modules:
  0.0 711.8 jit_solution(13096034925757239329)
XLA Ops:
  16.9 331.4 %while.36 = (s32[]{:T(128)}, bf16[2,128,128]{2,1,0:T(8,128)(2,1)S(1)}, f32[16,16384]{1,0:T(8,128)S(1)}, s32[32,8]{1,0:T(8,128)S(1)}, s32[32]{0:T(128)}, /*index=...) while((s32[]{:T(128)}, ...), condition=%wide.region_1.3_spmd.clone, body=%wide.region_0.0_spmd.clone.sunk | while | flops 59114820 | bytes 4592123 | solution.py:52
  59.6 5.3 collective-permute-done
  70.3 5.3 collective-permute-done
  81.1 5.3 collective-permute-done
  91.9 5.3 collective-permute-done
  102.6 5.3 collective-permute-done
  113.4 5.3 collective-permute-done
  124.2 5.3 collective-permute-done
  134.9 5.3 collective-permute-done
  145.7 5.3 collective-permute-done
  156.5 5.3 collective-permute-done
  167.3 5.3 collective-permute-done
  178.0 5.3 collective-permute-done
  188.8 5.3 collective-permute-done
  199.6 5.3 collective-permute-done
  210.3 5.3 collective-permute-done
  221.1 5.3 collective-permute-done
  231.9 5.3 collective-permute-done
  242.7 5.3 collective-permute-done
  253.4 5.3 collective-permute-done
  264.2 5.3 collective-permute-done
  275.0 5.3 collective-permute-done
  285.7 5.3 collective-permute-done
  296.5 5.3 collective-permute-done
  307.3 5.3 collective-permute-done
  318.0 5.3 collective-permute-done
  328.8 5.3 collective-permute-done
  349.6 12.0 %copy.20 = bf16[1,1,32,8,128,128]{4,5,3,2,1,0:T(8,128)(2,1)} copy(bf16[1,1,32,8,128,128]{5,4,3,2,1,0:T(8,128)(2,1)} %bitcast.84) | data formatting | bytes 16777216 | tf_op args[1]
  362.3 28.7 %reduce-scatter.2.cloned.1.call-done = f32[256,128]{1,0:T(8,128)} async-done(((f32[2048,128]{1,0:T(8,128)}), f32[256,128]{1,0:T(8,128)}) %reduce-scatter.2.cloned.1.call-update) | async-done | bytes 131088 | tf_op jit(solution)/shard_map/reduce_scatter | solution.py:53
  395.2 22.5 %all_gather.3 = bf16[2048,128]{1,0:T(8,128)(2,1)S(1)} all-gather(bf16[256,128]{1,0:T(8,128)(2,1)S(1)} %convolution_convert_fusion), channel_id=1, replica_groups=mesh['blk'=32,'rep'=8] {'rep'}, dimensions={0}, use_global_device_ids=true | all-gather | bytes 589824 | tf_op jit(solution)/shard_map/all_gather | solution.py:67
  420.7 282.0 %while.37 = (s32[]{:T(128)}, f32[2,16384]{1,0:T(2,128)S(1)}, s32[32,8]{1,0:T(8,128)S(1)}, s32[32]{0:T(128)S(1)}, bf16[32,8,128,128]{2,3,1,0:T(8,128)(2,1)}, /*in...) while((s32[]{:T(128)}, f32[2,16384]{1,0:T(2,128)S(1)}, ...), condition=%wide.region_4.7_spmd.clone, body=%wide.region_3.0_spmd.clone.sunk | while | flops 36865136 | bytes 2888324 | solution.py:85
  420.7 14.4 %collective-permute-start.1 = (f32[2,16384]{1,0:T(2,128)S(1)}, f32[2,16384]{1,0:T(2,128)S(1)}, u32[]{:S(2)}, u32[]{:S(2)}) collective-permute-start(f32[2,16384]{1,0:T(2,128)S(1)} %get-tuple-element.686), channel_id=1, source_target_pairs={{0,8},{8,16},{16,24},{24,32},{32,40},{40,48},{48,56},{56,64},{64,7... | collective-permute-start | bytes 393224 | tf_op jit(solution)/shard_map/while/body/eval_jaxpr/ppermute | solution.py:11
  (665 shorter events, 475.9 us)
Async XLA Ops:
  7.2 383.9 %reduce-scatter.2.cloned.1.call-start = ((), (), s32[]{:S(2)}) async-start(), calls=%async_computation.1 | async-start | bytes 1179648 | tf_op jit(solution)/shard_map/reduce_scatter | solution.py:53
  68.3 7.4 %collective-permute-start = (bf16[2,128,128]{2,1,0:T(8,128)(2,1)S(1)}, bf16[2,128,128]{2,1,0:T(8,128)(2,1)S(1)}, u32[]{:S(2)}, u32[]{:S(2)}) collective-permute-start(bf16[2,128,128]{2,1,0:T(8,128)(2,1)S(1)} %get-tuple-element.654), channel_id=1, source_target_pairs={{0,8},{8,16},{16,24},{24,32},{32,40},{40,48},{48,56},{56,64},{64,7... | collective-permute-start | bytes 196616 | tf_op jit(solution)/shard_map/while/body/eval_jaxpr/ppermute | solution.py:11
  349.5 353.9 %all-reduce.2.cloned.1.call-start = ((), (), s32[]{:S(2)}) async-start(), calls=%async_computation.2 | async-start | bytes 131072 | tf_op jit(solution)/shard_map/psum | solution.py:65
  420.7 17.6 %collective-permute-start.1 = (f32[2,16384]{1,0:T(2,128)S(1)}, f32[2,16384]{1,0:T(2,128)S(1)}, u32[]{:S(2)}, u32[]{:S(2)}) collective-permute-start(f32[2,16384]{1,0:T(2,128)S(1)} %get-tuple-element.686), channel_id=1, source_target_pairs={{0,8},{8,16},{16,24},{24,32},{32,40},{40,48},{48,56},{56,64},{64,7... | collective-permute-start | bytes 393224 | tf_op jit(solution)/shard_map/while/body/eval_jaxpr/ppermute | solution.py:11
  452.7 7.7 %collective-permute-start.1 = (f32[2,16384]{1,0:T(2,128)S(1)}, f32[2,16384]{1,0:T(2,128)S(1)}, u32[]{:S(2)}, u32[]{:S(2)}) collective-permute-start(f32[2,16384]{1,0:T(2,128)S(1)} %get-tuple-element.686), channel_id=1, source_target_pairs={{0,8},{8,16},{16,24},{24,32},{32,40},{40,48},{48,56},{56,64},{64,7... | collective-permute-start | bytes 393224 | tf_op jit(solution)/shard_map/while/body/eval_jaxpr/ppermute | solution.py:11
  461.3 8.1 %collective-permute-start.1 = (f32[2,16384]{1,0:T(2,128)S(1)}, f32[2,16384]{1,0:T(2,128)S(1)}, u32[]{:S(2)}, u32[]{:S(2)}) collective-permute-start(f32[2,16384]{1,0:T(2,128)S(1)} %get-tuple-element.686), channel_id=1, source_target_pairs={{0,8},{8,16},{16,24},{24,32},{32,40},{40,48},{48,56},{56,64},{64,7... | collective-permute-start | bytes 393224 | tf_op jit(solution)/shard_map/while/body/eval_jaxpr/ppermute | solution.py:11
  470.2 8.2 %collective-permute-start.1 = (f32[2,16384]{1,0:T(2,128)S(1)}, f32[2,16384]{1,0:T(2,128)S(1)}, u32[]{:S(2)}, u32[]{:S(2)}) collective-permute-start(f32[2,16384]{1,0:T(2,128)S(1)} %get-tuple-element.686), channel_id=1, source_target_pairs={{0,8},{8,16},{16,24},{24,32},{32,40},{40,48},{48,56},{56,64},{64,7... | collective-permute-start | bytes 393224 | tf_op jit(solution)/shard_map/while/body/eval_jaxpr/ppermute | solution.py:11
  479.2 8.1 %collective-permute-start.1 = (f32[2,16384]{1,0:T(2,128)S(1)}, f32[2,16384]{1,0:T(2,128)S(1)}, u32[]{:S(2)}, u32[]{:S(2)}) collective-permute-start(f32[2,16384]{1,0:T(2,128)S(1)} %get-tuple-element.686), channel_id=1, source_target_pairs={{0,8},{8,16},{16,24},{24,32},{32,40},{40,48},{48,56},{56,64},{64,7... | collective-permute-start | bytes 393224 | tf_op jit(solution)/shard_map/while/body/eval_jaxpr/ppermute | solution.py:11
  488.2 8.1 %collective-permute-start.1 = (f32[2,16384]{1,0:T(2,128)S(1)}, f32[2,16384]{1,0:T(2,128)S(1)}, u32[]{:S(2)}, u32[]{:S(2)}) collective-permute-start(f32[2,16384]{1,0:T(2,128)S(1)} %get-tuple-element.686), channel_id=1, source_target_pairs={{0,8},{8,16},{16,24},{24,32},{32,40},{40,48},{48,56},{56,64},{64,7... | collective-permute-start | bytes 393224 | tf_op jit(solution)/shard_map/while/body/eval_jaxpr/ppermute | solution.py:11
  497.1 8.1 %collective-permute-start.1 = (f32[2,16384]{1,0:T(2,128)S(1)}, f32[2,16384]{1,0:T(2,128)S(1)}, u32[]{:S(2)}, u32[]{:S(2)}) collective-permute-start(f32[2,16384]{1,0:T(2,128)S(1)} %get-tuple-element.686), channel_id=1, source_target_pairs={{0,8},{8,16},{16,24},{24,32},{32,40},{40,48},{48,56},{56,64},{64,7... | collective-permute-start | bytes 393224 | tf_op jit(solution)/shard_map/while/body/eval_jaxpr/ppermute | solution.py:11
  506.0 8.2 %collective-permute-start.1 = (f32[2,16384]{1,0:T(2,128)S(1)}, f32[2,16384]{1,0:T(2,128)S(1)}, u32[]{:S(2)}, u32[]{:S(2)}) collective-permute-start(f32[2,16384]{1,0:T(2,128)S(1)} %get-tuple-element.686), channel_id=1, source_target_pairs={{0,8},{8,16},{16,24},{24,32},{32,40},{40,48},{48,56},{56,64},{64,7... | collective-permute-start | bytes 393224 | tf_op jit(solution)/shard_map/while/body/eval_jaxpr/ppermute | solution.py:11
  515.0 8.1 %collective-permute-start.1 = (f32[2,16384]{1,0:T(2,128)S(1)}, f32[2,16384]{1,0:T(2,128)S(1)}, u32[]{:S(2)}, u32[]{:S(2)}) collective-permute-start(f32[2,16384]{1,0:T(2,128)S(1)} %get-tuple-element.686), channel_id=1, source_target_pairs={{0,8},{8,16},{16,24},{24,32},{32,40},{40,48},{48,56},{56,64},{64,7... | collective-permute-start | bytes 393224 | tf_op jit(solution)/shard_map/while/body/eval_jaxpr/ppermute | solution.py:11
  524.0 8.1 %collective-permute-start.1 = (f32[2,16384]{1,0:T(2,128)S(1)}, f32[2,16384]{1,0:T(2,128)S(1)}, u32[]{:S(2)}, u32[]{:S(2)}) collective-permute-start(f32[2,16384]{1,0:T(2,128)S(1)} %get-tuple-element.686), channel_id=1, source_target_pairs={{0,8},{8,16},{16,24},{24,32},{32,40},{40,48},{48,56},{56,64},{64,7... | collective-permute-start | bytes 393224 | tf_op jit(solution)/shard_map/while/body/eval_jaxpr/ppermute | solution.py:11
  532.9 8.1 %collective-permute-start.1 = (f32[2,16384]{1,0:T(2,128)S(1)}, f32[2,16384]{1,0:T(2,128)S(1)}, u32[]{:S(2)}, u32[]{:S(2)}) collective-permute-start(f32[2,16384]{1,0:T(2,128)S(1)} %get-tuple-element.686), channel_id=1, source_target_pairs={{0,8},{8,16},{16,24},{24,32},{32,40},{40,48},{48,56},{56,64},{64,7... | collective-permute-start | bytes 393224 | tf_op jit(solution)/shard_map/while/body/eval_jaxpr/ppermute | solution.py:11
  541.8 8.1 %collective-permute-start.1 = (f32[2,16384]{1,0:T(2,128)S(1)}, f32[2,16384]{1,0:T(2,128)S(1)}, u32[]{:S(2)}, u32[]{:S(2)}) collective-permute-start(f32[2,16384]{1,0:T(2,128)S(1)} %get-tuple-element.686), channel_id=1, source_target_pairs={{0,8},{8,16},{16,24},{24,32},{32,40},{40,48},{48,56},{56,64},{64,7... | collective-permute-start | bytes 393224 | tf_op jit(solution)/shard_map/while/body/eval_jaxpr/ppermute | solution.py:11
  550.8 8.1 %collective-permute-start.1 = (f32[2,16384]{1,0:T(2,128)S(1)}, f32[2,16384]{1,0:T(2,128)S(1)}, u32[]{:S(2)}, u32[]{:S(2)}) collective-permute-start(f32[2,16384]{1,0:T(2,128)S(1)} %get-tuple-element.686), channel_id=1, source_target_pairs={{0,8},{8,16},{16,24},{24,32},{32,40},{40,48},{48,56},{56,64},{64,7... | collective-permute-start | bytes 393224 | tf_op jit(solution)/shard_map/while/body/eval_jaxpr/ppermute | solution.py:11
  559.7 8.1 %collective-permute-start.1 = (f32[2,16384]{1,0:T(2,128)S(1)}, f32[2,16384]{1,0:T(2,128)S(1)}, u32[]{:S(2)}, u32[]{:S(2)}) collective-permute-start(f32[2,16384]{1,0:T(2,128)S(1)} %get-tuple-element.686), channel_id=1, source_target_pairs={{0,8},{8,16},{16,24},{24,32},{32,40},{40,48},{48,56},{56,64},{64,7... | collective-permute-start | bytes 393224 | tf_op jit(solution)/shard_map/while/body/eval_jaxpr/ppermute | solution.py:11
  568.7 8.1 %collective-permute-start.1 = (f32[2,16384]{1,0:T(2,128)S(1)}, f32[2,16384]{1,0:T(2,128)S(1)}, u32[]{:S(2)}, u32[]{:S(2)}) collective-permute-start(f32[2,16384]{1,0:T(2,128)S(1)} %get-tuple-element.686), channel_id=1, source_target_pairs={{0,8},{8,16},{16,24},{24,32},{32,40},{40,48},{48,56},{56,64},{64,7... | collective-permute-start | bytes 393224 | tf_op jit(solution)/shard_map/while/body/eval_jaxpr/ppermute | solution.py:11
  577.6 8.1 %collective-permute-start.1 = (f32[2,16384]{1,0:T(2,128)S(1)}, f32[2,16384]{1,0:T(2,128)S(1)}, u32[]{:S(2)}, u32[]{:S(2)}) collective-permute-start(f32[2,16384]{1,0:T(2,128)S(1)} %get-tuple-element.686), channel_id=1, source_target_pairs={{0,8},{8,16},{16,24},{24,32},{32,40},{40,48},{48,56},{56,64},{64,7... | collective-permute-start | bytes 393224 | tf_op jit(solution)/shard_map/while/body/eval_jaxpr/ppermute | solution.py:11
  586.6 8.1 %collective-permute-start.1 = (f32[2,16384]{1,0:T(2,128)S(1)}, f32[2,16384]{1,0:T(2,128)S(1)}, u32[]{:S(2)}, u32[]{:S(2)}) collective-permute-start(f32[2,16384]{1,0:T(2,128)S(1)} %get-tuple-element.686), channel_id=1, source_target_pairs={{0,8},{8,16},{16,24},{24,32},{32,40},{40,48},{48,56},{56,64},{64,7... | collective-permute-start | bytes 393224 | tf_op jit(solution)/shard_map/while/body/eval_jaxpr/ppermute | solution.py:11
  595.5 8.1 %collective-permute-start.1 = (f32[2,16384]{1,0:T(2,128)S(1)}, f32[2,16384]{1,0:T(2,128)S(1)}, u32[]{:S(2)}, u32[]{:S(2)}) collective-permute-start(f32[2,16384]{1,0:T(2,128)S(1)} %get-tuple-element.686), channel_id=1, source_target_pairs={{0,8},{8,16},{16,24},{24,32},{32,40},{40,48},{48,56},{56,64},{64,7... | collective-permute-start | bytes 393224 | tf_op jit(solution)/shard_map/while/body/eval_jaxpr/ppermute | solution.py:11
  604.4 8.1 %collective-permute-start.1 = (f32[2,16384]{1,0:T(2,128)S(1)}, f32[2,16384]{1,0:T(2,128)S(1)}, u32[]{:S(2)}, u32[]{:S(2)}) collective-permute-start(f32[2,16384]{1,0:T(2,128)S(1)} %get-tuple-element.686), channel_id=1, source_target_pairs={{0,8},{8,16},{16,24},{24,32},{32,40},{40,48},{48,56},{56,64},{64,7... | collective-permute-start | bytes 393224 | tf_op jit(solution)/shard_map/while/body/eval_jaxpr/ppermute | solution.py:11
  613.4 8.1 %collective-permute-start.1 = (f32[2,16384]{1,0:T(2,128)S(1)}, f32[2,16384]{1,0:T(2,128)S(1)}, u32[]{:S(2)}, u32[]{:S(2)}) collective-permute-start(f32[2,16384]{1,0:T(2,128)S(1)} %get-tuple-element.686), channel_id=1, source_target_pairs={{0,8},{8,16},{16,24},{24,32},{32,40},{40,48},{48,56},{56,64},{64,7... | collective-permute-start | bytes 393224 | tf_op jit(solution)/shard_map/while/body/eval_jaxpr/ppermute | solution.py:11
  622.3 8.1 %collective-permute-start.1 = (f32[2,16384]{1,0:T(2,128)S(1)}, f32[2,16384]{1,0:T(2,128)S(1)}, u32[]{:S(2)}, u32[]{:S(2)}) collective-permute-start(f32[2,16384]{1,0:T(2,128)S(1)} %get-tuple-element.686), channel_id=1, source_target_pairs={{0,8},{8,16},{16,24},{24,32},{32,40},{40,48},{48,56},{56,64},{64,7... | collective-permute-start | bytes 393224 | tf_op jit(solution)/shard_map/while/body/eval_jaxpr/ppermute | solution.py:11
  631.3 8.1 %collective-permute-start.1 = (f32[2,16384]{1,0:T(2,128)S(1)}, f32[2,16384]{1,0:T(2,128)S(1)}, u32[]{:S(2)}, u32[]{:S(2)}) collective-permute-start(f32[2,16384]{1,0:T(2,128)S(1)} %get-tuple-element.686), channel_id=1, source_target_pairs={{0,8},{8,16},{16,24},{24,32},{32,40},{40,48},{48,56},{56,64},{64,7... | collective-permute-start | bytes 393224 | tf_op jit(solution)/shard_map/while/body/eval_jaxpr/ppermute | solution.py:11
  640.3 8.1 %collective-permute-start.1 = (f32[2,16384]{1,0:T(2,128)S(1)}, f32[2,16384]{1,0:T(2,128)S(1)}, u32[]{:S(2)}, u32[]{:S(2)}) collective-permute-start(f32[2,16384]{1,0:T(2,128)S(1)} %get-tuple-element.686), channel_id=1, source_target_pairs={{0,8},{8,16},{16,24},{24,32},{32,40},{40,48},{48,56},{56,64},{64,7... | collective-permute-start | bytes 393224 | tf_op jit(solution)/shard_map/while/body/eval_jaxpr/ppermute | solution.py:11
  649.2 8.1 %collective-permute-start.1 = (f32[2,16384]{1,0:T(2,128)S(1)}, f32[2,16384]{1,0:T(2,128)S(1)}, u32[]{:S(2)}, u32[]{:S(2)}) collective-permute-start(f32[2,16384]{1,0:T(2,128)S(1)} %get-tuple-element.686), channel_id=1, source_target_pairs={{0,8},{8,16},{16,24},{24,32},{32,40},{40,48},{48,56},{56,64},{64,7... | collective-permute-start | bytes 393224 | tf_op jit(solution)/shard_map/while/body/eval_jaxpr/ppermute | solution.py:11
  658.1 8.1 %collective-permute-start.1 = (f32[2,16384]{1,0:T(2,128)S(1)}, f32[2,16384]{1,0:T(2,128)S(1)}, u32[]{:S(2)}, u32[]{:S(2)}) collective-permute-start(f32[2,16384]{1,0:T(2,128)S(1)} %get-tuple-element.686), channel_id=1, source_target_pairs={{0,8},{8,16},{16,24},{24,32},{32,40},{40,48},{48,56},{56,64},{64,7... | collective-permute-start | bytes 393224 | tf_op jit(solution)/shard_map/while/body/eval_jaxpr/ppermute | solution.py:11
  667.0 8.1 %collective-permute-start.1 = (f32[2,16384]{1,0:T(2,128)S(1)}, f32[2,16384]{1,0:T(2,128)S(1)}, u32[]{:S(2)}, u32[]{:S(2)}) collective-permute-start(f32[2,16384]{1,0:T(2,128)S(1)} %get-tuple-element.686), channel_id=1, source_target_pairs={{0,8},{8,16},{16,24},{24,32},{32,40},{40,48},{48,56},{56,64},{64,7... | collective-permute-start | bytes 393224 | tf_op jit(solution)/shard_map/while/body/eval_jaxpr/ppermute | solution.py:11
  675.9 8.1 %collective-permute-start.1 = (f32[2,16384]{1,0:T(2,128)S(1)}, f32[2,16384]{1,0:T(2,128)S(1)}, u32[]{:S(2)}, u32[]{:S(2)}) collective-permute-start(f32[2,16384]{1,0:T(2,128)S(1)} %get-tuple-element.686), channel_id=1, source_target_pairs={{0,8},{8,16},{16,24},{24,32},{32,40},{40,48},{48,56},{56,64},{64,7... | collective-permute-start | bytes 393224 | tf_op jit(solution)/shard_map/while/body/eval_jaxpr/ppermute | solution.py:11
  684.9 8.1 %collective-permute-start.1 = (f32[2,16384]{1,0:T(2,128)S(1)}, f32[2,16384]{1,0:T(2,128)S(1)}, u32[]{:S(2)}, u32[]{:S(2)}) collective-permute-start(f32[2,16384]{1,0:T(2,128)S(1)} %get-tuple-element.686), channel_id=1, source_target_pairs={{0,8},{8,16},{16,24},{24,32},{32,40},{40,48},{48,56},{56,64},{64,7... | collective-permute-start | bytes 393224 | tf_op jit(solution)/shard_map/while/body/eval_jaxpr/ppermute | solution.py:11
  693.8 8.1 %collective-permute-start.1 = (f32[2,16384]{1,0:T(2,128)S(1)}, f32[2,16384]{1,0:T(2,128)S(1)}, u32[]{:S(2)}, u32[]{:S(2)}) collective-permute-start(f32[2,16384]{1,0:T(2,128)S(1)} %get-tuple-element.686), channel_id=1, source_target_pairs={{0,8},{8,16},{16,24},{24,32},{32,40},{40,48},{48,56},{56,64},{64,7... | collective-permute-start | bytes 393224 | tf_op jit(solution)/shard_map/while/body/eval_jaxpr/ppermute | solution.py:11
  (36 other events, 770.7 us)
Sparse Core Ops, SparseCore 0:
  349.7 41.3 reduce-scatter.1
  397.2 242.5 all-reduce.1
where the time goes:
time: 720 us; the launch traced here: 712 us
  waiting for transfers between devices  312 us (43%)
  matrix products  158 us (22%)
  local copies, waits for them, and re-layouts  116 us (16%)
  other arithmetic  44.4 us (6%)
  starting transfers between devices  39.3 us (5%)
  blocking collectives  22.5 us (3%)
  between operations  14.2 us (2%)
    ppermute x62, waiting for transfers between devices, passed_along(): lax.ppermute(array, axis, [(i, (i + by) % devices) for i in range(devices)])  284 us
    dynamic_slice x62, local copies, waits for them, and re-layouts, live_of(): return (slot_ids < counts[s]).astype(jnp.float32)  56.7 us
    dot_general x32, matrix products, forward_term(): jnp.dot(placing, product.reshape(capacity, -1), precision=lax.Precision.H...  47.6 us
    convert_element_type x64, other arithmetic, live_of(): return (slot_ids < counts[s]).astype(jnp.float32)  41.4 us
    dot_general x32, matrix products, backward_term(): jnp.einsum('ktu,ktf->kuf', own_tiles[s], rows_sel, preferred_element_type...  40.1 us
    dot_general x32, matrix products, forward_term(): jnp.einsum('ktu,kuf->ktf', own_tiles[s], picked, preferred_element_type=j...  40 us
    ppermute x62, starting transfers between devices, passed_along(): lax.ppermute(array, axis, [(i, (i + by) % devices) for i in range(devices)])  39.2 us
    reduce_scatter x1, waiting for transfers between devices, body(): lax.psum_scatter(partial_value.reshape(block_tiles * tile_len, feature_le...  28.7 us
  transfers between devices with their start and end apart: 64, of which 59 were waited for; matrix products, arithmetic and copies ran while one was open for 28% of the time, Pallas kernels for 0%

commit v1 on v0

v1 whole, which is shorter than its diff:
```python
import functools
import math

import jax
import jax.numpy as jnp
from jax import lax
from jax.experimental import pallas as pl
from jax.experimental.pallas import tpu as pltpu
from jax.sharding import PartitionSpec as P

MESH = pl.DeviceIdType.MESH
F32 = jnp.float32
BF16 = jnp.bfloat16
HIGHEST = lax.Precision.HIGHEST


def kernel(
    blocks, reps, node_total,
    features, tiles_hbm, counts, dst, src, dst_vec, weight, bias, cotangent,
    act_out, grad_out, wgrad_out,
    tiles, feats, chain, links_vec, links,
    part, part_in, grads_t, wterm, wrep, wquad, wz, wall,
    sib_out, sib_in, own_sum, z_in, y_in,
    tile_sem, link_sem, ag_send, ag_recv, rs_send, rs_recv, g_send, g_recv,
    w_send, w1_recv, w2_recv, w3_recv, w4_recv,
    sib_send, sib_recv, z_send, z_recv, y_send, y_recv,
):
    nz = blocks // 4
    half = nz // 2
    cap = dst.shape[1]
    tile = tiles.shape[1]
    feat = features.shape[1]
    n_slots = blocks * cap
    b = lax.axis_index("blk")
    r = lax.axis_index("rep")
    core = lax.rem(b, 2)
    yh = lax.rem(b // 2, 2)
    z = b // 4
    sib = b + 1 - 2 * core
    partner = b + 2 - 4 * yh
    diag = sib + 2 - 4 * yh
    up = lax.rem(b + 4, blocks)
    down = lax.rem(b + blocks - 4, blocks)

    sent = []

    def send(src_ref, dst_ref, send_sem, recv_sem, blk, rep):
        copy = pltpu.make_async_remote_copy(
            src_ref=src_ref, dst_ref=dst_ref, send_sem=send_sem, recv_sem=recv_sem,
            device_id=(blk, rep), device_id_type=MESH,
        )
        copy.start()
        sent.append(copy)

    def arrived(dst_ref, recv_sem):
        pltpu.make_async_remote_copy(
            src_ref=dst_ref, dst_ref=dst_ref, send_sem=w_send.at[0], recv_sem=recv_sem,
            device_id=(sib, r), device_id_type=MESH,
        ).wait_recv()

    tile_copy = pltpu.make_async_copy(tiles_hbm, tiles, tile_sem)
    tile_copy.start()

    z_peers = [lax.rem(b + 4 * i, blocks) for i in range(1, nz)]
    rep_peers = [lax.rem(r + i, reps) for i in range(1, reps)]
    barrier = pltpu.get_barrier_semaphore()
    for blk in [sib, partner, diag] + z_peers:
        pl.semaphore_signal(barrier, inc=1, device_id=(blk, r), device_id_type=MESH)
    for rep in rep_peers:
        pl.semaphore_signal(barrier, inc=1, device_id=(b, rep), device_id_type=MESH)
    feats[b] = features[...]
    pl.semaphore_wait(barrier, 3 + len(z_peers) + len(rep_peers))

    ag_count = [0]

    def pass_on(u, targets):
        for blk in targets:
            send(feats.at[u], feats.at[u], ag_send.at[ag_count[0]], ag_recv.at[u], blk, r)
            ag_count[0] += 1

    pass_on(b, [partner, up, down, sib])

    def step_of(n):
        group, j = n // 4, lax.rem(n, 4)
        dist = (group + 1) // 2
        zoff = lax.rem(jnp.where(lax.rem(group, 2) == 1, nz - dist, dist), nz)
        return lax.rem(z + zoff, nz) * 4 + j

    dst_tab = dst_vec[...]
    slot_iota = lax.broadcasted_iota(jnp.int32, dst_tab.shape, 0) * cap + lax.broadcasted_iota(
        jnp.int32, dst_tab.shape, 1
    )
    tile_iota = lax.broadcasted_iota(jnp.int32, (8, 128), 1)

    def link_step(n, carry):
        current, before, last = carry
        s = lax.rem(b - step_of(n) + blocks, blocks)
        for k in range(cap):
            to = jnp.where(k < counts[s], dst[s, k], -1)
            before = jnp.where(slot_iota == s * cap + k, current, before)
            current = jnp.where(dst_tab == to, n * cap + k, current)
            last = jnp.where(tile_iota == to, n * cap + k, last)
        return current, before, last

    nothing = jnp.full(dst_tab.shape, n_slots, jnp.int32)
    current, before, last = lax.fori_loop(
        0, blocks, link_step, (nothing, nothing, jnp.full((8, 128), n_slots, jnp.int32))
    )
    links_vec[...] = jnp.zeros(links_vec.shape, jnp.int32)
    links_vec[0:blocks, 0:cap] = before
    links_vec[blocks:blocks + 8, :] = last
    link_copy = pltpu.make_async_copy(links_vec, links, link_sem)
    link_copy.start()
    chain[n_slots] = jnp.zeros((tile, feat), F32)

    def z_unit(zoff, y, c):
        return lax.rem(z + zoff + nz, nz) * 4 + 2 * y + c

    arrived(feats.at[partner], ag_recv.at[partner])
    pass_on(partner, [up, down, sib])

    link_copy.wait()
    tile_copy.wait()

    def forward_steps(first, last_step):
        def one(n, carry):
            u = step_of(n)
            s = lax.rem(b - u + blocks, blocks)
            seen = feats[u]
            both = jnp.concatenate([seen[:tile], seen[tile:]], axis=1)
            for k in range(cap):
                product = jnp.dot(tiles[s * cap + k], both, preferred_element_type=F32)
                use_second = jnp.full((tile, feat), src[s, k], jnp.int32) == 1
                term = jnp.where(use_second, product[:, feat:], product[:, :feat])
                chain[n * cap + k] = term + chain[links[s, k]]
            return carry

        lax.fori_loop(first, last_step, one, 0)

    def own_core_units(d):
        if d < half:
            return [(-d, 0, up), (d, 0, down), (-d, 1, up), (d, 1, down)]
        return [(half, 0, up), (half, 1, down)]

    for d in range(half + 1):
        if d >= 1:
            for zoff, y, target in own_core_units(d):
                u = z_unit(zoff, y, core)
                arrived(feats.at[u], ag_recv.at[u])
                go_on = d + 1 < half or (d + 1 == half and (y == 0) == (zoff < 0))
                pass_on(u, [target, sib] if go_on else [sib])
        if d >= 1:
            wait_d = d - 1
            if wait_d == 0:
                others = [sib, diag]
            else:
                others = [z_unit(zoff, y, 1 - core) for zoff, y, _ in own_core_units(wait_d)]
            for u in others:
                arrived(feats.at[u], ag_recv.at[u])
            if wait_d == 0:
                forward_steps(0, 4)
            else:
                forward_steps(8 * wait_d - 4, 8 * wait_d + 4)
    for zoff, y, _ in own_core_units(half):
        u = z_unit(zoff, y, 1 - core)
        arrived(feats.at[u], ag_recv.at[u])
    forward_steps(8 * half - 4, 8 * half)

    def partial_of(t):
        return chain[links[blocks, t]]

    for i, rep in enumerate(rep_peers):
        for j in range(2):
            part[rep, j * tile:(j + 1) * tile] = partial_of(rep * 2 + j)
        send(part.at[rep], part_in.at[r], rs_send.at[i], rs_recv.at[r], b, rep)
    aggregate = jnp.concatenate([partial_of(r * 2), partial_of(r * 2 + 1)], axis=0)
    for rep in rep_peers:
        arrived(part_in.at[rep], rs_recv.at[rep])
        aggregate = aggregate + part_in[rep]

    pre_act = jnp.dot(aggregate, weight[...], precision=HIGHEST, preferred_element_type=F32) + bias[...]
    sigma = jax.nn.sigmoid(pre_act)
    act_out[...] = pre_act * sigma
    pre_grad = cotangent[...] * sigma * (1.0 + pre_act * (1.0 - sigma))
    agg_grad_t = lax.dot_general(
        weight[...], pre_grad, (((1,), (1,)), ((), ())), precision=HIGHEST, preferred_element_type=F32
    ).astype(BF16)
    for j in range(2):
        grads_t[2 * r + j] = agg_grad_t[:, j * tile:(j + 1) * tile]
    for i, rep in enumerate(rep_peers):
        mine = grads_t.at[pl.ds(2 * r, 2)]
        send(mine, mine, g_send.at[i], g_recv.at[r], b, rep)

    wterm[...] = lax.dot_general(
        aggregate, pre_grad, (((0,), (0,)), ((), ())), precision=HIGHEST, preferred_element_type=F32
    ) * (1.0 / math.sqrt(node_total))
    w_rows = feat // reps
    w_count = [0]

    def w_send_to(src_ref, dst_ref, recv_sem, blk, rep):
        send(src_ref, dst_ref, w_send.at[w_count[0]], recv_sem, blk, rep)
        w_count[0] += 1

    for rep in rep_peers:
        w_send_to(wterm.at[pl.ds(rep * w_rows, w_rows)], wrep.at[r], w1_recv.at[r], b, rep)
    for rep in rep_peers:
        theirs = grads_t.at[pl.ds(2 * rep, 2)]
        arrived(theirs, g_recv.at[rep])

    def w_stage(stage):
        if stage == 0:
            total = wterm[pl.ds(r * w_rows, w_rows)]
            for rep in rep_peers:
                arrived(wrep.at[rep], w1_recv.at[rep])
                total = total + wrep[rep]
            place = lax.rem(b, 4)
            wquad[place] = total
            for blk in [sib, partner, diag]:
                w_send_to(wquad.at[place], wquad.at[place], w2_recv.at[place], blk, r)
        elif stage == 1:
            for blk in [sib, partner, diag]:
                place = lax.rem(blk, 4)
                arrived(wquad.at[place], w2_recv.at[place])
            total = wquad[0]
            for i in range(1, 4):
                total = total + wquad[i]
            wz[z] = total
            for blk in z_peers:
                w_send_to(wz.at[z], wz.at[z], w3_recv.at[z], blk, r)
        elif stage == 2:
            for blk in z_peers:
                arrived(wz.at[blk // 4], w3_recv.at[blk // 4])
            total = wz[0]
            for i in range(1, nz):
                total = total + wz[i]
            wall[r] = total
            for rep in rep_peers:
                w_send_to(wall.at[r], wall.at[r], w4_recv.at[r], b, rep)
        else:
            for rep in rep_peers:
                arrived(wall.at[rep], w4_recv.at[rep])
            wgrad_out[...] = wall[...].reshape(feat, feat)

    def backward_unit(u):
        s = lax.rem(b - u + blocks, blocks)
        first, second = [], []
        for k in range(cap):
            rows = grads_t[dst[s, k]]
            side = jnp.full(rows.shape, jnp.where(k < counts[s], src[s, k], 2), jnp.int32)
            first.append(jnp.where(side == 0, rows, jnp.zeros_like(rows)))
            second.append(jnp.where(side == 1, rows, jnp.zeros_like(rows)))
        picked = jnp.concatenate(
            [jnp.concatenate(first, axis=1), jnp.concatenate(second, axis=1)], axis=0
        )
        stacked = tiles[pl.ds(s * cap, cap)].reshape(cap * tile, tile)
        return jnp.dot(picked, stacked, preferred_element_type=F32)

    index = [0]
    z_count = [0]
    for dist in range(half, -1, -1):
        if dist == half:
            entries = [(half, 0, 0), (half, 1, 1)]
        elif dist >= 1:
            entries = [(dist, 0, 0), (-dist, 0, 1), (dist, 1, 0), (-dist, 1, 1)]
        else:
            entries = [(0, 0, None), (0, 1, None)]
        slots = []
        for zoff, y, way in entries:
            i = index[0]
            index[0] += 1
            slots.append(i)
            sib_out[i] = backward_unit(z_unit(zoff, y, 1 - core))
            send(sib_out.at[i], sib_in.at[i], sib_send.at[i], sib_recv.at[i], sib, r)
        for i, (zoff, y, way) in zip(slots, entries):
            total = backward_unit(z_unit(zoff, y, core))
            arrived(sib_in.at[i], sib_recv.at[i])
            total = total + sib_in[i]
            if dist == 0:
                ways = [0, 1]
            elif dist == half:
                ways = []
            else:
                ways = [way]
            for w in ways:
                if dist == half - 1 and w != y:
                    continue
                arrived(z_in.at[w, dist, y], z_recv.at[w, dist, y])
                total = total + z_in[w, dist, y]
            own_sum[i] = total
            if dist >= 1:
                target = up if way == 0 else down
                send(
                    own_sum.at[i], z_in.at[way, dist - 1, y],
                    z_send.at[z_count[0]], z_recv.at[way, dist - 1, y], target, r,
                )
                z_count[0] += 1
        if half - dist < 4:
            w_stage(half - dist)
    for stage in range(half + 1, 4):
        w_stage(stage)
    base = index[0] - 2
    send(own_sum.at[base + 1 - yh], y_in, y_send, y_recv, partner, r)
    arrived(y_in, y_recv)
    grad_out[...] = own_sum[base + yh] + y_in[...]

    for copy in sent:
        copy.wait_send()


def body(features, adj_tiles, tile_counts, dst_tile, src_tile, weight, bias_term, cotangent):
    blocks = lax.axis_size("blk")
    reps = lax.axis_size("rep")
    steps, cap, tile = adj_tiles.shape[2:5]
    rows, feat = features.shape
    node_total = rows * blocks * reps
    n_slots = steps * cap
    nz = blocks // 4
    half = nz // 2
    w_rows = feat // reps
    dst = dst_tile[0, 0]
    vmem = pl.BlockSpec(memory_space=pltpu.VMEM)
    smem = pl.BlockSpec(memory_space=pltpu.SMEM)
    dma = pltpu.SemaphoreType.DMA
    act, grad_t, wgrad = pl.pallas_call(
        functools.partial(kernel, blocks, reps, node_total),
        out_shape=(
            jax.ShapeDtypeStruct((rows, feat), F32),
            jax.ShapeDtypeStruct((rows, feat), F32),
            jax.ShapeDtypeStruct((feat, feat), F32),
        ),
        in_specs=[vmem, pl.BlockSpec(memory_space=pl.ANY), smem, smem, smem, vmem, vmem, vmem, vmem],
        out_specs=(vmem, vmem, vmem),
        scratch_shapes=[
            pltpu.VMEM((n_slots, tile, tile), BF16),
            pltpu.VMEM((blocks, rows, feat), BF16),
            pltpu.VMEM((n_slots + 1, tile, feat), F32),
            pltpu.VMEM((blocks + 8, 128), jnp.int32),
            pltpu.SMEM((blocks + 8, 128), jnp.int32),
            pltpu.VMEM((reps, rows, feat), F32),
            pltpu.VMEM((reps, rows, feat), F32),
            pltpu.VMEM((2 * reps, feat, tile), BF16),
            pltpu.VMEM((feat, feat), F32),
            pltpu.VMEM((reps, w_rows, feat), F32),
            pltpu.VMEM((4, w_rows, feat), F32),
            pltpu.VMEM((nz, w_rows, feat), F32),
            pltpu.VMEM((reps, w_rows, feat), F32),
            pltpu.VMEM((blocks // 2, 2 * feat, tile), F32),
            pltpu.VMEM((blocks // 2, 2 * feat, tile), F32),
            pltpu.VMEM((blocks // 2, 2 * feat, tile), F32),
            pltpu.VMEM((2, half, 2, 2 * feat, tile), F32),
            pltpu.VMEM((2 * feat, tile), F32),
            dma, dma,
            dma((blocks,)), dma((blocks,)),
            dma((reps,)), dma((reps,)),
            dma((reps,)), dma((reps,)),
            dma((2 * reps + nz + 4,)), dma((reps,)), dma((4,)), dma((nz,)), dma((reps,)),
            dma((blocks // 2,)), dma((blocks // 2,)),
            dma((2 * nz,)), dma((2, half, 2)),
            dma, dma,
        ],
        compiler_params=pltpu.CompilerParams(
            collective_id=0, has_side_effects=True, vmem_limit_bytes=58 * 1024 * 1024
        ),
        cost_estimate=pl.CostEstimate(
            flops=4 * n_slots * tile * tile * feat,
            bytes_accessed=n_slots * tile * tile * 2,
            transcendentals=rows * feat,
        ),
        name="graph_layer",
    )(
        features, adj_tiles.reshape(n_slots, tile, tile), tile_counts[0, 0], dst, src_tile[0, 0],
        dst, weight, bias_term.reshape(1, feat), cotangent,
    )
    feature_grad = jnp.swapaxes(grad_t.reshape(2, feat, tile), 1, 2).reshape(rows, feat)
    return act, feature_grad, wgrad


def solution(mesh):
    in_specs = (
        P(("blk", "rep"), None),
        P("blk", "rep", None, None, None, None),
        P("blk", "rep", None),
        P("blk", "rep", None, None),
        P("blk", "rep", None, None),
        P(),
        P(),
        P(("blk", "rep"), None),
    )
    out_specs = (P(("blk", "rep"), None), P(("blk", "rep"), None), P())
    return jax.shard_map(body, mesh=mesh, in_specs=in_specs, out_specs=out_specs, check_vma=False)
```

time: 720 us -> 100 us (0.14); the launches traced: 712 us -> 99.8 us
  waiting for transfers between devices: 312 us -> 0 us
  matrix products: 158 us -> 0 us
  local copies, waits for them, and re-layouts: 116 us -> 7.43 us
  Pallas kernels: 0 us -> 91.7 us
  other arithmetic: 44.4 us -> 0 us
  starting transfers between devices: 39.3 us -> 0 us
  blocking collectives: 22.5 us -> 0 us
  between operations: 14.2 us -> 0.64 us
    ppermute x62 -> x0, waiting for transfers between devices: 284 us -> none  [passed_along(): lax.ppermute(array, axis, [(i, (i + by) % devices) for i in range(devices)])]
    dot_general x131 -> x0, matrix products: 158 us -> none  [the longest x32 47.6 us: forward_term(): jnp.dot(placing, product.reshape(capacity, -1), precision=lax.Precision.H...]
    pallas_call x0 -> x1, Pallas kernels: none -> 91.7 us  [body(): pl.pallas_call(functools.partial(kernel, blocks, reps, node_total), out_s...]
    dynamic_slice x62 -> x0, local copies, waits for them, and re-layouts: 56.7 us -> none  [live_of(): return (slot_ids < counts[s]).astype(jnp.float32)]
    convert_element_type x64 -> x0, other arithmetic: 41.4 us -> none  [live_of(): return (slot_ids < counts[s]).astype(jnp.float32)]
    ppermute x62 -> x0, starting transfers between devices: 39.2 us -> none  [passed_along(): lax.ppermute(array, axis, [(i, (i + by) % devices) for i in range(devices)])]
    gather x64 -> x0, local copies, waits for them, and re-layouts: 38.2 us -> none  [the longest x32 19.1 us: backward_term(): rows_sel = jnp.take(block_grad, dst_ids[s], axis=0)]
    reduce_scatter x1 -> x0, waiting for transfers between devices: 28.7 us -> none  [body(): lax.psum_scatter(partial_value.reshape(block_tiles * tile_len, feature_le...]
  transfers between devices with their start and end apart: 64 -> 0, of which waited for: 59 -> 0; matrix products, arithmetic and copies ran while one was open for 28% -> 0% of each run, Pallas kernels for 0% -> 0%
where the time goes in v1:
time: 100 us; the launch traced here: 99.8 us
  Pallas kernels  91.7 us (92%)
  local copies, waits for them, and re-layouts  7.43 us (7%)
    pallas_call x1, Pallas kernels, body(): pl.pallas_call(functools.partial(kernel, blocks, reps, node_total), out_s...  91.7 us
    unnamed x4, local copies, waits for them, and re-layouts  5.77 us

profile of v1, /device:TPU:1, one launch (start us, length us, event | category | flops | bytes accessed | tf_op | source)
XLA Modules:
  0.0 99.8 jit_solution(8789949472546340127)
XLA Ops:
  0.6 1.4 %copy.11 = s32[1,1,32,8]{3,2,1,0:T(8,128)} copy(s32[1,1,32,8]{2,3,1,0:T(8,128)} %param.11) | data formatting | bytes 2048 | tf_op args[3]
  2.0 1.4 %copy.12 = s32[1,1,32,8]{3,2,1,0:T(8,128)} copy(s32[1,1,32,8]{2,3,1,0:T(8,128)} %param.12) | data formatting | bytes 2048 | tf_op args[4]
  3.4 91.7 %graph_layer.1 = (f32[256,128]{1,0:T(8,128)}, f32[256,128]{1,0:T(8,128)}, f32[128,128]{1,0:T(8,128)}) custom-call(bf16[256,128]{1,0:T(8,128)(2,1)} %features.1, bf16[256,128,128]{2,1,0:T(8,128)(2,1)} %bitcast.9, s32[32]{0:T(128)} %bitcast.15, s32[32,8]{1,0:T(8,128)} %bitcast.10, s32[32,8]{1,0:T(8,128)} %bitcast.14, s32[32,8]{1,0:T(8,128)} %bitcast.11, ...), custom_call_target="tpu_custom_call" | custom-call | flops 2147483648 | bytes 8388608 | tf_op jit(solution)/shard_map/graph_layer/pallas_call | solution.py:324
  95.1 1.7 %copy.13 = f32[2,128,128]{2,1,0:T(8,128)} copy(f32[2,128,128]{1,2,0:T(8,128)} %bitcast.13) | data formatting | bytes 262144 | tf_op jit(solution)/shard_map/transpose | solution.py:374
  96.8 1.6 %copy.16 = f32[256,128]{1,0:T(8,128)} copy(f32[256,128]{1,0:T(8,128)} %get-tuple-element.12) | data formatting | bytes 262144
  98.3 1.5 %copy.17 = f32[128,128]{1,0:T(8,128)} copy(f32[128,128]{1,0:T(8,128)} %get-tuple-element.14) | data formatting | bytes 131072

commit v2 on v1

v2 whole, which is shorter than its diff:
```python
import functools
import math

import jax
import jax.numpy as jnp
from jax import lax
from jax.experimental import pallas as pl
from jax.experimental.pallas import tpu as pltpu
from jax.sharding import PartitionSpec as P

MESH = pl.DeviceIdType.MESH
F32 = jnp.float32
BF16 = jnp.bfloat16
HIGHEST = lax.Precision.HIGHEST
I16 = jnp.int16
SCALE_ROWS = 16
PIECES = 2


def encode(ref, value):
    rows = value.shape[0]
    largest = jnp.max(jnp.abs(value), axis=0, keepdims=True)
    power = jnp.clip(jnp.floor(14.9 - jnp.log2(largest)), -120.0, 120.0)
    ref[0:rows] = jnp.round(value * jnp.exp2(power)).astype(jnp.int32).astype(I16)
    ref[rows:rows + SCALE_ROWS] = jnp.broadcast_to(
        power.astype(jnp.int32), (SCALE_ROWS, value.shape[1])
    ).astype(I16)


def decode(ref):
    rows = ref.shape[0] - SCALE_ROWS
    scale = jnp.exp2(-ref[rows:rows + SCALE_ROWS].astype(jnp.int32).astype(F32))
    value = ref[0:rows].astype(jnp.int32).astype(F32)
    grouped = value.reshape(rows // SCALE_ROWS, SCALE_ROWS, value.shape[1]) * scale[None]
    return grouped.reshape(value.shape)


def kernel(
    blocks, reps, node_total,
    features, tiles_hbm, counts_hbm, dst_hbm, src_hbm, weight_hbm, bias_hbm, cotangent_hbm,
    act_out, grad_out, wgrad_out,
    counts, dst, src, dst_vec, weight, bias, cotangent, tiles, feats, chain, links_vec, links,
    part, part_in, grads_t, wterm, wrep, wquad, wz, wall,
    sib_out, sib_in, own_sum, z_out, z_in, y_in,
    in_sems, tile_sem, link_sem, ag_send, ag_recv, rs_send, rs_recv, g_send, g_recv,
    w_send, w1_recv, w2_recv, w3_recv, w4_recv,
    sib_send, sib_recv, z_send, z_recv, y_recv,
):
    nz = blocks // 4
    half = nz // 2
    cap = dst.shape[0]
    tile = tiles.shape[1]
    feat = features.shape[1]
    n_slots = blocks * cap
    b = lax.axis_index("blk")
    r = lax.axis_index("rep")
    core = lax.rem(b, 2)
    yh = lax.rem(b // 2, 2)
    z = b // 4
    sib = b + 1 - 2 * core
    partner = b + 2 - 4 * yh
    diag = sib + 2 - 4 * yh
    up = lax.rem(b + 4, blocks)
    down = lax.rem(b + blocks - 4, blocks)

    sent = []

    def send(src_ref, dst_ref, send_sem, recv_sem, blk, rep):
        copy = pltpu.make_async_remote_copy(
            src_ref=src_ref, dst_ref=dst_ref, send_sem=send_sem, recv_sem=recv_sem,
            device_id=(blk, rep), device_id_type=MESH,
        )
        copy.start()
        sent.append(copy)

    def arrived(dst_ref, recv_sem):
        pltpu.make_async_remote_copy(
            src_ref=dst_ref, dst_ref=dst_ref, send_sem=w_send.at[0], recv_sem=recv_sem,
            device_id=(sib, r), device_id_type=MESH,
        ).wait_recv()

    z_peers = [lax.rem(b + 4 * i, blocks) for i in range(1, nz)]
    rep_peers = [lax.rem(r + i, reps) for i in range(1, reps)]
    partner_up = lax.rem(partner + 4, blocks)
    partner_down = lax.rem(partner + blocks - 4, blocks)
    blk_peers = [sib, partner, diag, partner_up, partner_down] + z_peers
    barrier = pltpu.get_barrier_semaphore()
    for blk in blk_peers:
        pl.semaphore_signal(barrier, inc=1, device_id=(blk, r), device_id_type=MESH)
    for rep in rep_peers:
        pl.semaphore_signal(barrier, inc=1, device_id=(b, rep), device_id_type=MESH)
    copies = [
        pltpu.make_async_copy(from_ref, to_ref, in_sems.at[i])
        for i, (from_ref, to_ref) in enumerate([
            (features, feats.at[b]), (dst_hbm, dst_vec), (dst_hbm, dst), (counts_hbm, counts),
            (src_hbm, src), (weight_hbm, weight), (bias_hbm, bias), (cotangent_hbm, cotangent),
        ])
    ]
    own_copy, index_copies, dense_copies = copies[0], copies[1:5], copies[5:]
    own_copy.start()
    for copy in index_copies:
        copy.start()
    tile_copy = pltpu.make_async_copy(tiles_hbm, tiles, tile_sem)
    tile_copy.start()
    for copy in dense_copies:
        copy.start()
    pl.semaphore_wait(barrier, len(blk_peers) + len(rep_peers))

    ag_count = [0]
    piece = features.shape[0] // PIECES

    def pass_on(u, target, first, n_rows, flag):
        rows = feats.at[u, pl.ds(first, n_rows)]
        send(rows, rows, ag_send.at[ag_count[0]], ag_recv.at[u, flag], target, r)
        ag_count[0] += 1

    def to_sibling(u):
        pass_on(u, sib, 0, PIECES * piece, 0)

    def unit_arrived(u):
        arrived(feats.at[u], ag_recv.at[u, 0])

    own_copy.wait()
    for targets in ((up, down), (partner_up, partner_down, partner)):
        for h in range(PIECES):
            for target in targets:
                pass_on(b, target, h * piece, piece, h)
    to_sibling(b)
    for copy in index_copies:
        copy.wait()

    groups = [("own", 0)]
    for d in range(1, half + 1):
        groups += [("own", d), ("other", d)]
        if d == 1:
            groups.append(("other", 0))

    def group_size(group):
        return 2 if group[1] in (0, half) else 4

    starts = {}
    total_steps = 0
    for group in groups:
        starts[group] = total_steps
        total_steps += group_size(group)

    def unit_in(group, j):
        which, d = group
        y = yh if which == "own" else 1 - yh
        if group_size(group) == 2:
            zoff, c = d, j
        else:
            zoff, c = nz + d * (2 * lax.rem(j, 2) - 1), j // 2
        return lax.rem(z + zoff, nz) * 4 + 2 * y + lax.rem(core + c, 2)

    dst_tab = dst_vec[...]
    slot_iota = lax.broadcasted_iota(jnp.int32, dst_tab.shape, 1) * cap + lax.broadcasted_iota(
        jnp.int32, dst_tab.shape, 0
    )
    tile_iota = lax.broadcasted_iota(jnp.int32, (8, 128), 1)

    def link_step(group, j, carry):
        current, before, last = carry
        n = starts[group] + j
        s = lax.rem(b - unit_in(group, j) + blocks, blocks)
        for k in range(cap):
            to = jnp.where(k < counts[s], dst[k, s], -1)
            before = jnp.where(slot_iota == s * cap + k, current, before)
            current = jnp.where(dst_tab == to, n * cap + k, current)
            last = jnp.where(tile_iota == to, n * cap + k, last)
        return current, before, last

    nothing = jnp.full(dst_tab.shape, n_slots, jnp.int32)
    carry = (nothing, nothing, jnp.full((8, 128), n_slots, jnp.int32))
    for group in groups:
        carry = lax.fori_loop(0, group_size(group), functools.partial(link_step, group), carry)
    _, before, last = carry
    links_vec[...] = jnp.zeros(links_vec.shape, jnp.int32)
    links_vec[0:cap, 0:blocks] = before
    links_vec[8:16, :] = last
    link_copy = pltpu.make_async_copy(links_vec, links, link_sem)
    link_copy.start()
    chain[n_slots] = jnp.zeros((tile, feat), F32)

    def z_unit(zoff, y, c):
        return lax.rem(z + zoff + nz, nz) * 4 + 2 * y + c

    def z_unit(zoff, y, c):
        return lax.rem(z + zoff + nz, nz) * 4 + 2 * y + c

    def take_in(group):
        which, d = group
        y = yh if which == "own" else 1 - yh
        if d in (0, half):
            moves = [(d, None)]
        else:
            moves = [
                (zoff, target if d + 1 < half or which == last_y else None)
                for zoff, target, last_y in ((-d, up, "own"), (d, down, "other"))
            ]
        for h in range(PIECES):
            for zoff, target in moves:
                u = z_unit(zoff, y, core)
                arrived(feats.at[u, pl.ds(h * piece, piece)], ag_recv.at[u, h])
                if target is not None:
                    pass_on(u, target, h * piece, piece, h)
        for zoff, _ in moves:
            to_sibling(z_unit(zoff, y, core))

    def work_on(group):
        which, d = group
        y = yh if which == "own" else 1 - yh
        for zoff in (d,) if d in (0, half) else (-d, d):
            unit_arrived(z_unit(zoff, y, 1 - core))

        def one(j, carry):
            u = unit_in(group, j)
            n = starts[group] + j
            s = lax.rem(b - u + blocks, blocks)
            seen = feats[u]
            both = jnp.concatenate([seen[:tile], seen[tile:]], axis=1)
            for k in range(cap):
                product = jnp.dot(tiles[s * cap + k], both, preferred_element_type=F32)
                use_second = jnp.full((tile, feat), src[k, s], jnp.int32) == 1
                term = jnp.where(use_second, product[:, feat:], product[:, :feat])
                chain[n * cap + k] = term + chain[links[k, s]]
            return carry

        lax.fori_loop(0, group_size(group), one, 0)

    for i, group in enumerate(groups):
        if i == len(groups) - 1:
            work_on(groups[i - 2])
        if i >= 1:
            take_in(group)
        if i == 1:
            link_copy.wait()
            tile_copy.wait()
        if 2 <= i < len(groups) - 1:
            work_on(groups[i - 2])
    work_on(groups[-2])
    work_on(groups[-1])

    def partial_of(t):
        return chain[links[8, t]]

    for i, rep in enumerate(rep_peers):
        encode(part.at[rep], jnp.concatenate([partial_of(rep * 2), partial_of(rep * 2 + 1)], axis=0))
        send(part.at[rep], part_in.at[r], rs_send.at[i], rs_recv.at[r], b, rep)
    aggregate = jnp.concatenate([partial_of(r * 2), partial_of(r * 2 + 1)], axis=0)
    for copy in dense_copies:
        copy.wait()
    for rep in rep_peers:
        arrived(part_in.at[rep], rs_recv.at[rep])
        aggregate = aggregate + decode(part_in.at[rep])

    pre_act = jnp.dot(aggregate, weight[...], precision=HIGHEST, preferred_element_type=F32) + bias[...]
    sigma = jax.nn.sigmoid(pre_act)
    pre_grad = cotangent[...] * sigma * (1.0 + pre_act * (1.0 - sigma))
    agg_grad_t = lax.dot_general(
        weight[...], pre_grad, (((1,), (1,)), ((), ())), precision=HIGHEST, preferred_element_type=F32
    ).astype(BF16)
    for j in range(2):
        grads_t[2 * r + j] = agg_grad_t[:, j * tile:(j + 1) * tile]
    for i, rep in enumerate(rep_peers):
        mine = grads_t.at[pl.ds(2 * r, 2)]
        send(mine, mine, g_send.at[i], g_recv.at[r], b, rep)

    act_out[...] = pre_act * sigma

    wterm[...] = lax.dot_general(
        aggregate, pre_grad, (((0,), (0,)), ((), ())), precision=HIGHEST, preferred_element_type=F32
    ) * (1.0 / math.sqrt(node_total))
    w_rows = feat // reps
    w_count = [0]

    def w_send_to(src_ref, dst_ref, recv_sem, blk, rep):
        send(src_ref, dst_ref, w_send.at[w_count[0]], recv_sem, blk, rep)
        w_count[0] += 1

    for rep in rep_peers:
        w_send_to(wterm.at[pl.ds(rep * w_rows, w_rows)], wrep.at[r], w1_recv.at[r], b, rep)
    for rep in rep_peers:
        theirs = grads_t.at[pl.ds(2 * rep, 2)]
        arrived(theirs, g_recv.at[rep])

    w_done = [0]

    def w_stage(stage):
        w_done[0] += 1
        if stage == 0:
            total = wterm[pl.ds(r * w_rows, w_rows)]
            for rep in rep_peers:
                arrived(wrep.at[rep], w1_recv.at[rep])
                total = total + wrep[rep]
            place = lax.rem(b, 4)
            wquad[place] = total
            for blk in [sib, partner, diag]:
                w_send_to(wquad.at[place], wquad.at[place], w2_recv.at[place], blk, r)
        elif stage == 1:
            for blk in [sib, partner, diag]:
                place = lax.rem(blk, 4)
                arrived(wquad.at[place], w2_recv.at[place])
            total = wquad[0]
            for i in range(1, 4):
                total = total + wquad[i]
            wz[z] = total
            for blk in z_peers:
                w_send_to(wz.at[z], wz.at[z], w3_recv.at[z], blk, r)
        elif stage == 2:
            for blk in z_peers:
                arrived(wz.at[blk // 4], w3_recv.at[blk // 4])
            total = wz[0]
            for i in range(1, nz):
                total = total + wz[i]
            wall[r] = total
            for rep in rep_peers:
                w_send_to(wall.at[r], wall.at[r], w4_recv.at[r], b, rep)
        else:
            for rep in rep_peers:
                arrived(wall.at[rep], w4_recv.at[rep])
            wgrad_out[...] = wall[...].reshape(feat, feat)

    def backward_unit(u):
        s = lax.rem(b - u + blocks, blocks)
        first, second = [], []
        for k in range(cap):
            rows = grads_t[dst[k, s]]
            side = jnp.full(rows.shape, jnp.where(k < counts[s], src[k, s], 2), jnp.int32)
            first.append(jnp.where(side == 0, rows, jnp.zeros_like(rows)))
            second.append(jnp.where(side == 1, rows, jnp.zeros_like(rows)))
        picked = jnp.concatenate(
            [jnp.concatenate(first, axis=1), jnp.concatenate(second, axis=1)], axis=0
        )
        stacked = tiles[pl.ds(s * cap, cap)].reshape(cap * tile, tile)
        return jnp.dot(picked, stacked, preferred_element_type=F32)

    index = 0
    for dist in range(half, -1, -1):
        if dist == half:
            entries = [(half, 0, [], 0), (half, 1, [], 1)]
            if half > 1:
                entries += [(half - 1, 1, [], 0), (1 - half, 0, [], 1)]
        elif dist == half - 1 and dist >= 1:
            entries = [(dist, 0, [0], 0), (-dist, 1, [1], 1)]
        elif dist >= 1:
            entries = [
                (zoff, y, [way], way) for y in range(2) for way, zoff in enumerate((dist, -dist))
            ]
        else:
            entries = [(0, 1, [0, 1] if half > 1 else [1], None)]
        if dist == min(2, half):
            entries.append((0, 0, [], None))
        units = [(index + i, zoff, (yh + 1 - y) % 2) for i, (zoff, y, _, _) in enumerate(entries)]
        index += len(entries)
        for i, zoff, y in units:
            encode(sib_out.at[i], backward_unit(z_unit(zoff, y, 1 - core)))
            send(sib_out.at[i], sib_in.at[i], sib_send.at[i], sib_recv.at[i], sib, r)
        for i, zoff, y in units:
            own_sum[i] = backward_unit(z_unit(zoff, y, core))
        if dist < half - 1 and w_done[0] < 3:
            w_stage(w_done[0])
        for i, _, _ in units:
            arrived(sib_in.at[i], sib_recv.at[i])
            own_sum[i] = own_sum[i] + decode(sib_in.at[i])
        for (i, _, _), (zoff, y, ways, way) in zip(units, entries):
            for j in range(2):
                value = own_sum[i, j * feat:(j + 1) * feat]
                for w in ways:
                    arrived(z_in.at[w, abs(zoff), y, j], z_recv.at[w, abs(zoff), y, j])
                    value = value + decode(z_in.at[w, abs(zoff), y, j])
                if zoff == 0 and y == 1:
                    for k in range(3):
                        arrived(y_in.at[k, j], y_recv.at[k, j])
                        value = value + decode(y_in.at[k, j])
                    grad_out[j * feat:(j + 1) * feat] = value
                    continue
                out = z_out.at[i, j]
                encode(out, value)
                if zoff == 0:
                    target, place, flag = partner, y_in.at[2, j], y_recv.at[2, j]
                elif abs(zoff) == 1 and y == 0:
                    target = partner_up if way == 0 else partner_down
                    place, flag = y_in.at[way, j], y_recv.at[way, j]
                else:
                    target = up if way == 0 else down
                    near = abs(zoff) - 1
                    place, flag = z_in.at[way, near, y, j], z_recv.at[way, near, y, j]
                send(out, place, z_send.at[i, j], flag, target, r)
        if dist == half:
            w_stage(0)
    for stage in range(w_done[0], 4):
        w_stage(stage)

    for copy in sent:
        copy.wait_send()


def finish(act, grad_t, wgrad, act_out, grad_out, wgrad_out):
    act_out[...] = act[...]
    wgrad_out[...] = wgrad[...]
    feat = wgrad.shape[0]
    tile = grad_t.shape[1]
    for j in range(2):
        grad_out[j * tile:(j + 1) * tile] = grad_t[j * feat:(j + 1) * feat].T


def body(features, adj_tiles, tile_counts, dst_tile, src_tile, weight, bias_term, cotangent):
    blocks = lax.axis_size("blk")
    reps = lax.axis_size("rep")
    steps, cap, tile = adj_tiles.shape[2:5]
    rows, feat = features.shape
    node_total = rows * blocks * reps
    n_slots = steps * cap
    nz = blocks // 4
    half = nz // 2
    w_rows = feat // reps
    dst = dst_tile[0, 0].T
    src = src_tile[0, 0].T
    shapes = (
        jax.ShapeDtypeStruct((rows, feat), F32),
        jax.ShapeDtypeStruct((rows, feat), F32),
        jax.ShapeDtypeStruct((feat, feat), F32),
    )
    vmem = pl.BlockSpec(memory_space=pltpu.VMEM)
    dma = pltpu.SemaphoreType.DMA
    act, grad_t, wgrad = pl.pallas_call(
        functools.partial(kernel, blocks, reps, node_total),
        out_shape=shapes,
        in_specs=[pl.BlockSpec(memory_space=pltpu.HBM)] * 8,
        out_specs=(vmem, vmem, vmem),
        scratch_shapes=[
            pltpu.SMEM((blocks,), jnp.int32),
            pltpu.SMEM((cap, blocks), jnp.int32),
            pltpu.SMEM((cap, blocks), jnp.int32),
            pltpu.VMEM((cap, blocks), jnp.int32),
            pltpu.VMEM((feat, feat), F32),
            pltpu.VMEM((1, feat), F32),
            pltpu.VMEM((rows, feat), F32),
            pltpu.VMEM((n_slots, tile, tile), BF16),
            pltpu.VMEM((blocks, rows, feat), BF16),
            pltpu.VMEM((n_slots + 1, tile, feat), F32),
            pltpu.VMEM((16, 128), jnp.int32),
            pltpu.SMEM((16, 128), jnp.int32),
            pltpu.VMEM((reps, rows + SCALE_ROWS, feat), I16),
            pltpu.VMEM((reps, rows + SCALE_ROWS, feat), I16),
            pltpu.VMEM((2 * reps, feat, tile), BF16),
            pltpu.VMEM((feat, feat), F32),
            pltpu.VMEM((reps, w_rows, feat), F32),
            pltpu.VMEM((4, w_rows, feat), F32),
            pltpu.VMEM((nz, w_rows, feat), F32),
            pltpu.VMEM((reps, w_rows, feat), F32),
            pltpu.VMEM((blocks // 2, 2 * feat + SCALE_ROWS, tile), I16),
            pltpu.VMEM((blocks // 2, 2 * feat + SCALE_ROWS, tile), I16),
            pltpu.VMEM((blocks // 2, 2 * feat, tile), F32),
            pltpu.VMEM((blocks // 2, 2, feat + SCALE_ROWS, tile), I16),
            pltpu.VMEM((2, half, 2, 2, feat + SCALE_ROWS, tile), I16),
            pltpu.VMEM((3, 2, feat + SCALE_ROWS, tile), I16),
            dma((8,)), dma, dma,
            dma((PIECES * 2 * blocks,)), dma((blocks, PIECES)),
            dma((reps,)), dma((reps,)),
            dma((reps,)), dma((reps,)),
            dma((2 * reps + nz + 4,)), dma((reps,)), dma((4,)), dma((nz,)), dma((reps,)),
            dma((blocks // 2,)), dma((blocks // 2,)),
            dma((blocks // 2, 2)), dma((2, half, 2, 2)),
            dma((3, 2)),
        ],
        compiler_params=pltpu.CompilerParams(
            collective_id=0, has_side_effects=True, vmem_limit_bytes=58 * 1024 * 1024
        ),
        cost_estimate=pl.CostEstimate(
            flops=4 * n_slots * tile * tile * feat,
            bytes_accessed=n_slots * tile * tile * 2,
            transcendentals=rows * feat,
        ),
        name="graph_layer",
    )(
        features, adj_tiles.reshape(n_slots, tile, tile), tile_counts[0, 0], dst, src,
        weight, bias_term.reshape(1, feat), cotangent,
    )
    return pl.pallas_call(finish, out_shape=shapes, name="outputs")(act, grad_t, wgrad)


def solution(mesh):
    in_specs = (
        P(("blk", "rep"), None),
        P("blk", "rep", None, None, None, None),
        P("blk", "rep", None),
        P("blk", "rep", None, None),
        P("blk", "rep", None, None),
        P(),
        P(),
        P(("blk", "rep"), None),
    )
    out_specs = (P(("blk", "rep"), None), P(("blk", "rep"), None), P())
    return jax.shard_map(body, mesh=mesh, in_specs=in_specs, out_specs=out_specs, check_vma=False)
```

time: 100 us -> 75.8 us (0.76)
  Pallas kernels: 91.7 us -> 74.9 us
  local copies, waits for them, and re-layouts: 7.43 us -> 0 us
    pallas_call x1, Pallas kernels: 91.7 us -> 73.2 us  [body(): pl.pallas_call(functools.partial(kernel, blocks, reps, node_total), out_s...]
    unnamed x4 -> x0, local copies, waits for them, and re-layouts: 5.77 us -> none
    pallas_call x0 -> x1, Pallas kernels: none -> 1.74 us  [body(): pl.pallas_call(finish, out_shape=shapes, name='outputs')(act, grad_t, wgrad)]
    transpose x1 -> x0, local copies, waits for them, and re-layouts: 1.66 us -> none  [body(): jnp.swapaxes(grad_t.reshape(2, feat, tile), 1, 2).reshape(rows, feat)]
where the time goes in v2:
time: 75.8 us; the launch traced here: 75.6 us
  Pallas kernels  74.9 us (99%)
    pallas_call x1, Pallas kernels, body(): pl.pallas_call(functools.partial(kernel, blocks, reps, node_total), out_s...  73.2 us
    pallas_call x1, Pallas kernels, body(): pl.pallas_call(finish, out_shape=shapes, name='outputs')(act, grad_t, wgrad)  1.74 us

profile of v2, /device:TPU:1, one launch (start us, length us, event | category | flops | bytes accessed | tf_op | source)
XLA Modules:
  0.0 75.6 jit_solution(1144986859210582225)
XLA Ops:
  0.6 73.2 %graph_layer.1 = (f32[256,128]{1,0:T(8,128)}, f32[256,128]{1,0:T(8,128)}, f32[128,128]{1,0:T(8,128)}) custom-call(bf16[256,128]{1,0:T(8,128)(2,1)} %features.1, bf16[256,128,128]{2,1,0:T(8,128)(2,1)} %bitcast.9, s32[32]{0:T(128)} %bitcast.12, s32[8,32]{1,0:T(8,128)} %bitcast.10, s32[8,32]{1,0:T(8,128)} %bitcast.11, f32[128,128]{1,0:T(8,128)} %weight_hbm.1, ...), custom_call_target="tpu_custom_call" | custom-call | flops 2147483648 | bytes 8388608 | tf_op jit(solution)/shard_map/graph_layer/pallas_call | solution.py:427
  73.8 1.7 %outputs.1 = (f32[256,128]{1,0:T(8,128)}, f32[256,128]{1,0:T(8,128)}, f32[128,128]{1,0:T(8,128)}) custom-call(f32[256,128]{1,0:T(8,128)} %get-tuple-element.6.act, f32[256,128]{1,0:T(8,128)} %get-tuple-element.7.grad_t, f32[128,128]{1,0:T(8,128)} %get-tuple-element.8.wgrad), custom_call_target="tpu_custom_call" | custom-call | tf_op jit(solution)/shard_map/outputs/pallas_call | solution.py:481

commit v3 on v2

--- a/solution.py
+++ b/solution.py
@@ -14,7 +14,7 @@
 HIGHEST = lax.Precision.HIGHEST
 I16 = jnp.int16
 SCALE_ROWS = 16
-PIECES = 2
+PIECES = 1
 
 
 def encode(ref, value):
@@ -73,6 +73,10 @@
         copy.start()
         sent.append(copy)
 
+    def settle(keep=0):
+        while len(sent) > keep:
+            sent.pop(0).wait_send()
+
     def arrived(dst_ref, recv_sem):
         pltpu.make_async_remote_copy(
             src_ref=dst_ref, dst_ref=dst_ref, send_sem=w_send.at[0], recv_sem=recv_sem,
@@ -182,15 +186,15 @@
     link_copy.start()
     chain[n_slots] = jnp.zeros((tile, feat), F32)
 
+    other_y = 1 - yh
+    z_base = {zoff: lax.rem(z + zoff + nz, nz) * 4 for zoff in range(1 - half, half + 1)}
+
     def z_unit(zoff, y, c):
-        return lax.rem(z + zoff + nz, nz) * 4 + 2 * y + c
-
-    def z_unit(zoff, y, c):
-        return lax.rem(z + zoff + nz, nz) * 4 + 2 * y + c
+        return z_base[zoff] + 2 * y + c
 
     def take_in(group):
         which, d = group
-        y = yh if which == "own" else 1 - yh
+        y = yh if which == "own" else other_y
         if d in (0, half):
             moves = [(d, None)]
         else:
@@ -209,7 +213,7 @@
 
     def work_on(group):
         which, d = group
-        y = yh if which == "own" else 1 - yh
+        y = yh if which == "own" else other_y
         for zoff in (d,) if d in (0, half) else (-d, d):
             unit_arrived(z_unit(zoff, y, 1 - core))
 
@@ -244,32 +248,40 @@
     def partial_of(t):
         return chain[links[8, t]]
 
-    for i, rep in enumerate(rep_peers):
-        encode(part.at[rep], jnp.concatenate([partial_of(rep * 2), partial_of(rep * 2 + 1)], axis=0))
-        send(part.at[rep], part_in.at[r], rs_send.at[i], rs_recv.at[r], b, rep)
-    aggregate = jnp.concatenate([partial_of(r * 2), partial_of(r * 2 + 1)], axis=0)
+    for j in range(2):
+        for i, rep in enumerate(rep_peers):
+            encode(part.at[rep, j], partial_of(rep * 2 + j))
+            send(part.at[rep, j], part_in.at[r, j], rs_send.at[i, j], rs_recv.at[r, j], b, rep)
+    settle(2 * len(rep_peers))
     for copy in dense_copies:
         copy.wait()
-    for rep in rep_peers:
-        arrived(part_in.at[rep], rs_recv.at[rep])
-        aggregate = aggregate + decode(part_in.at[rep])
-
-    pre_act = jnp.dot(aggregate, weight[...], precision=HIGHEST, preferred_element_type=F32) + bias[...]
-    sigma = jax.nn.sigmoid(pre_act)
-    pre_grad = cotangent[...] * sigma * (1.0 + pre_act * (1.0 - sigma))
-    agg_grad_t = lax.dot_general(
-        weight[...], pre_grad, (((1,), (1,)), ((), ())), precision=HIGHEST, preferred_element_type=F32
-    ).astype(BF16)
+    terms = []
     for j in range(2):
-        grads_t[2 * r + j] = agg_grad_t[:, j * tile:(j + 1) * tile]
-    for i, rep in enumerate(rep_peers):
-        mine = grads_t.at[pl.ds(2 * r, 2)]
-        send(mine, mine, g_send.at[i], g_recv.at[r], b, rep)
-
-    act_out[...] = pre_act * sigma
-
-    wterm[...] = lax.dot_general(
-        aggregate, pre_grad, (((0,), (0,)), ((), ())), precision=HIGHEST, preferred_element_type=F32
+        aggregate = partial_of(r * 2 + j)
+        for rep in rep_peers:
+            arrived(part_in.at[rep, j], rs_recv.at[rep, j])
+            aggregate = aggregate + decode(part_in.at[rep, j])
+        rows = slice(j * tile, (j + 1) * tile)
+        pre_act = jnp.dot(
+            aggregate, weight[...], precision=HIGHEST, preferred_element_type=F32
+        ) + bias[...]
+        sigma = jax.nn.sigmoid(pre_act)
+        pre_grad = cotangent[rows] * sigma * (1.0 + pre_act * (1.0 - sigma))
+        grads_t[2 * r + j] = lax.dot_general(
+            weight[...], pre_grad, (((1,), (1,)), ((), ())),
+            precision=HIGHEST, preferred_element_type=F32,
+        ).astype(BF16)
+        mine = grads_t.at[2 * r + j]
+        for i, rep in enumerate(rep_peers):
+            send(mine, mine, g_send.at[i, j], g_recv.at[r, j], b, rep)
+        act_out[rows] = pre_act * sigma
+        terms.append((aggregate, pre_grad))
+
+    wterm[...] = sum(
+        lax.dot_general(
+            aggregate, pre_grad, (((0,), (0,)), ((), ())), precision=HIGHEST, preferred_element_type=F32
+        )
+        for aggregate, pre_grad in terms
     ) * (1.0 / math.sqrt(node_total))
     w_rows = feat // reps
     w_count = [0]
@@ -280,9 +292,10 @@
 
     for rep in rep_peers:
         w_send_to(wterm.at[pl.ds(rep * w_rows, w_rows)], wrep.at[r], w1_recv.at[r], b, rep)
+    settle(3 * len(rep_peers))
     for rep in rep_peers:
-        theirs = grads_t.at[pl.ds(2 * rep, 2)]
-        arrived(theirs, g_recv.at[rep])
+        for j in range(2):
+            arrived(grads_t.at[2 * rep + j], g_recv.at[rep, j])
 
     w_done = [0]
 
@@ -351,7 +364,7 @@
             entries = [(0, 1, [0, 1] if half > 1 else [1], None)]
         if dist == min(2, half):
             entries.append((0, 0, [], None))
-        units = [(index + i, zoff, (yh + 1 - y) % 2) for i, (zoff, y, _, _) in enumerate(entries)]
+        units = [(index + i, zoff, yh if y else other_y) for i, (zoff, y, _, _) in enumerate(entries)]
         index += len(entries)
         for i, zoff, y in units:
             encode(sib_out.at[i], backward_unit(z_unit(zoff, y, 1 - core)))
@@ -360,40 +373,40 @@
             own_sum[i] = backward_unit(z_unit(zoff, y, core))
         if dist < half - 1 and w_done[0] < 3:
             w_stage(w_done[0])
+        if dist == 0:
+            settle(8)
         for i, _, _ in units:
             arrived(sib_in.at[i], sib_recv.at[i])
             own_sum[i] = own_sum[i] + decode(sib_in.at[i])
         for (i, _, _), (zoff, y, ways, way) in zip(units, entries):
-            for j in range(2):
-                value = own_sum[i, j * feat:(j + 1) * feat]
-                for w in ways:
-                    arrived(z_in.at[w, abs(zoff), y, j], z_recv.at[w, abs(zoff), y, j])
-                    value = value + decode(z_in.at[w, abs(zoff), y, j])
-                if zoff == 0 and y == 1:
-                    for k in range(3):
-                        arrived(y_in.at[k, j], y_recv.at[k, j])
-                        value = value + decode(y_in.at[k, j])
-                    grad_out[j * feat:(j + 1) * feat] = value
-                    continue
-                out = z_out.at[i, j]
-                encode(out, value)
-                if zoff == 0:
-                    target, place, flag = partner, y_in.at[2, j], y_recv.at[2, j]
-                elif abs(zoff) == 1 and y == 0:
-                    target = partner_up if way == 0 else partner_down
-                    place, flag = y_in.at[way, j], y_recv.at[way, j]
-                else:
-                    target = up if way == 0 else down
-                    near = abs(zoff) - 1
-                    place, flag = z_in.at[way, near, y, j], z_recv.at[way, near, y, j]
-                send(out, place, z_send.at[i, j], flag, target, r)
+            value = own_sum[i]
+            for w in ways:
+                arrived(z_in.at[w, abs(zoff), y], z_recv.at[w, abs(zoff), y])
+                value = value + decode(z_in.at[w, abs(zoff), y])
+            if zoff == 0 and y == 1:
+                for k in range(3):
+                    arrived(y_in.at[k], y_recv.at[k])
+                    value = value + decode(y_in.at[k])
+                grad_out[...] = value
+                continue
+            out = z_out.at[i]
+            encode(out, value)
+            if zoff == 0:
+                target, place, flag = partner, y_in.at[2], y_recv.at[2]
+            elif abs(zoff) == 1 and y == 0:
+                target = partner_up if way == 0 else partner_down
+                place, flag = y_in.at[way], y_recv.at[way]
+            else:
+                target = up if way == 0 else down
+                near = abs(zoff) - 1
+                place, flag = z_in.at[way, near, y], z_recv.at[way, near, y]
+            send(out, place, z_send.at[i], flag, target, r)
         if dist == half:
             w_stage(0)
     for stage in range(w_done[0], 4):
         w_stage(stage)
 
-    for copy in sent:
-        copy.wait_send()
+    settle()
 
 
 def finish(act, grad_t, wgrad, act_out, grad_out, wgrad_out):
@@ -442,8 +455,8 @@
             pltpu.VMEM((n_slots + 1, tile, feat), F32),
             pltpu.VMEM((16, 128), jnp.int32),
             pltpu.SMEM((16, 128), jnp.int32),
-            pltpu.VMEM((reps, rows + SCALE_ROWS, feat), I16),
-            pltpu.VMEM((reps, rows + SCALE_ROWS, feat), I16),
+            pltpu.VMEM((reps, 2, tile + SCALE_ROWS, feat), I16),
+            pltpu.VMEM((reps, 2, tile + SCALE_ROWS, feat), I16),
             pltpu.VMEM((2 * reps, feat, tile), BF16),
             pltpu.VMEM((feat, feat), F32),
             pltpu.VMEM((reps, w_rows, feat), F32),
@@ -453,17 +466,17 @@
             pltpu.VMEM((blocks // 2, 2 * feat + SCALE_ROWS, tile), I16),
             pltpu.VMEM((blocks // 2, 2 * feat + SCALE_ROWS, tile), I16),
             pltpu.VMEM((blocks // 2, 2 * feat, tile), F32),
-            pltpu.VMEM((blocks // 2, 2, feat + SCALE_ROWS, tile), I16),
-            pltpu.VMEM((2, half, 2, 2, feat + SCALE_ROWS, tile), I16),
-            pltpu.VMEM((3, 2, feat + SCALE_ROWS, tile), I16),
+            pltpu.VMEM((blocks // 2, 2 * feat + SCALE_ROWS, tile), I16),
+            pltpu.VMEM((2, half, 2, 2 * feat + SCALE_ROWS, tile), I16),
+            pltpu.VMEM((3, 2 * feat + SCALE_ROWS, tile), I16),
             dma((8,)), dma, dma,
             dma((PIECES * 2 * blocks,)), dma((blocks, PIECES)),
-            dma((reps,)), dma((reps,)),
-            dma((reps,)), dma((reps,)),
+            dma((reps, 2)), dma((reps, 2)),
+            dma((reps, 2)), dma((reps, 2)),
             dma((2 * reps + nz + 4,)), dma((reps,)), dma((4,)), dma((nz,)), dma((reps,)),
             dma((blocks // 2,)), dma((blocks // 2,)),
-            dma((blocks // 2, 2)), dma((2, half, 2, 2)),
-            dma((3, 2)),
+            dma((blocks // 2,)), dma((2, half, 2)),
+            dma((3,)),
         ],
         compiler_params=pltpu.CompilerParams(
             collective_id=0, has_side_effects=True, vmem_limit_bytes=58 * 1024 * 1024

time: 75.8 us -> 71.3 us (0.941)
  Pallas kernels: 74.9 us -> 70.3 us
    pallas_call x1, Pallas kernels: 73.2 us -> 68.5 us  [body(): pl.pallas_call(functools.partial(kernel, blocks, reps, node_total), out_s...]
where the time goes in v3:
time: 71.3 us; the launch traced here: 70.9 us
  Pallas kernels  70.3 us (99%)
    pallas_call x1, Pallas kernels, body(): pl.pallas_call(functools.partial(kernel, blocks, reps, node_total), out_s...  68.5 us
    pallas_call x1, Pallas kernels, body(): pl.pallas_call(finish, out_shape=shapes, name='outputs')(act, grad_t, wgrad)  1.74 us

profile of v3, /device:TPU:1, one launch (start us, length us, event | category | flops | bytes accessed | tf_op | source)
XLA Modules:
  0.0 70.9 jit_solution(4559891576557279107)
XLA Ops:
  0.6 68.5 %graph_layer.1 = (f32[256,128]{1,0:T(8,128)}, f32[256,128]{1,0:T(8,128)}, f32[128,128]{1,0:T(8,128)}) custom-call(bf16[256,128]{1,0:T(8,128)(2,1)} %features.1, bf16[256,128,128]{2,1,0:T(8,128)(2,1)} %bitcast.9, s32[32]{0:T(128)} %bitcast.12, s32[8,32]{1,0:T(8,128)} %bitcast.10, s32[8,32]{1,0:T(8,128)} %bitcast.11, f32[128,128]{1,0:T(8,128)} %weight_hbm.1, ...), custom_call_target="tpu_custom_call" | custom-call | flops 2147483648 | bytes 8388608 | tf_op jit(solution)/shard_map/graph_layer/pallas_call | solution.py:440
  69.2 1.7 %outputs.1 = (f32[256,128]{1,0:T(8,128)}, f32[256,128]{1,0:T(8,128)}, f32[128,128]{1,0:T(8,128)}) custom-call(f32[256,128]{1,0:T(8,128)} %get-tuple-element.6.act, f32[256,128]{1,0:T(8,128)} %get-tuple-element.7.grad_t, f32[128,128]{1,0:T(8,128)} %get-tuple-element.8.wgrad), custom_call_target="tpu_custom_call" | custom-call | tf_op jit(solution)/shard_map/outputs/pallas_call | solution.py:494

commit v4 on v3

--- a/solution.py
+++ b/solution.py
@@ -84,7 +84,14 @@
         ).wait_recv()
 
     z_peers = [lax.rem(b + 4 * i, blocks) for i in range(1, nz)]
-    rep_peers = [lax.rem(r + i, reps) for i in range(1, reps)]
+    n_x = reps // 2
+    steps_away = sorted(
+        ((dx, dy) for dx in range(n_x) for dy in range(2) if dx + dy),
+        key=lambda step: (-min(step[0], n_x - step[0]) - step[1], -step[1], step[0]),
+    )
+    rep_peers = [
+        lax.rem(r // n_x + dy, 2) * n_x + lax.rem(lax.rem(r, n_x) + dx, n_x) for dx, dy in steps_away
+    ]
     partner_up = lax.rem(partner + 4, blocks)
     partner_down = lax.rem(partner + blocks - 4, blocks)
     blk_peers = [sib, partner, diag, partner_up, partner_down] + z_peers
@@ -369,16 +376,22 @@
         for i, zoff, y in units:
             encode(sib_out.at[i], backward_unit(z_unit(zoff, y, 1 - core)))
             send(sib_out.at[i], sib_in.at[i], sib_send.at[i], sib_recv.at[i], sib, r)
-        for i, zoff, y in units:
-            own_sum[i] = backward_unit(z_unit(zoff, y, core))
         if dist < half - 1 and w_done[0] < 3:
             w_stage(w_done[0])
         if dist == 0:
             settle(8)
-        for i, _, _ in units:
-            arrived(sib_in.at[i], sib_recv.at[i])
-            own_sum[i] = own_sum[i] + decode(sib_in.at[i])
+        batch = 2 if dist == half else len(units)
+        ready = 0
         for (i, _, _), (zoff, y, ways, way) in zip(units, entries):
+            if ready == 0:
+                ready = batch
+                coming = units[i - units[0][0]:][:batch]
+                for m, m_zoff, m_y in coming:
+                    own_sum[m] = backward_unit(z_unit(m_zoff, m_y, core))
+                for m, _, _ in coming:
+                    arrived(sib_in.at[m], sib_recv.at[m])
+                    own_sum[m] = own_sum[m] + decode(sib_in.at[m])
+            ready -= 1
             value = own_sum[i]
             for w in ways:
                 arrived(z_in.at[w, abs(zoff), y], z_recv.at[w, abs(zoff), y])

time: 71.3 us -> 70.3 us (0.986)
  Pallas kernels: 70.3 us -> 69.5 us
    pallas_call x1, Pallas kernels: 68.5 us -> 67.8 us  [body(): pl.pallas_call(functools.partial(kernel, blocks, reps, node_total), out_s...]
where the time goes in v4:
time: 70.3 us; the launch traced here: 70.2 us
  Pallas kernels  69.5 us (99%)
    pallas_call x1, Pallas kernels, body(): pl.pallas_call(functools.partial(kernel, blocks, reps, node_total), out_s...  67.8 us
    pallas_call x1, Pallas kernels, body(): pl.pallas_call(finish, out_shape=shapes, name='outputs')(act, grad_t, wgrad)  1.74 us

profile of v4, /device:TPU:1, one launch (start us, length us, event | category | flops | bytes accessed | tf_op | source)
XLA Modules:
  0.0 70.2 jit_solution(200640041043695337)
XLA Ops:
  0.6 67.8 %graph_layer.1 = (f32[256,128]{1,0:T(8,128)}, f32[256,128]{1,0:T(8,128)}, f32[128,128]{1,0:T(8,128)}) custom-call(bf16[256,128]{1,0:T(8,128)(2,1)} %features.1, bf16[256,128,128]{2,1,0:T(8,128)(2,1)} %bitcast.9, s32[32]{0:T(128)} %bitcast.12, s32[8,32]{1,0:T(8,128)} %bitcast.10, s32[8,32]{1,0:T(8,128)} %bitcast.11, f32[128,128]{1,0:T(8,128)} %weight_hbm.1, ...), custom_call_target="tpu_custom_call" | custom-call | flops 2147483648 | bytes 8388608 | tf_op jit(solution)/shard_map/graph_layer/pallas_call | solution.py:453
  68.4 1.7 %outputs.1 = (f32[256,128]{1,0:T(8,128)}, f32[256,128]{1,0:T(8,128)}, f32[128,128]{1,0:T(8,128)}) custom-call(f32[256,128]{1,0:T(8,128)} %get-tuple-element.6.act, f32[256,128]{1,0:T(8,128)} %get-tuple-element.7.grad_t, f32[128,128]{1,0:T(8,128)} %get-tuple-element.8.wgrad), custom_call_target="tpu_custom_call" | custom-call | tf_op jit(solution)/shard_map/outputs/pallas_call | solution.py:507

commit v5 on v4

--- a/solution.py
+++ b/solution.py
@@ -380,7 +380,7 @@
             w_stage(w_done[0])
         if dist == 0:
             settle(8)
-        batch = 2 if dist == half else len(units)
+        batch = 2
         ready = 0
         for (i, _, _), (zoff, y, ways, way) in zip(units, entries):
             if ready == 0:
@@ -393,13 +393,14 @@
                     own_sum[m] = own_sum[m] + decode(sib_in.at[m])
             ready -= 1
             value = own_sum[i]
+            if zoff == 0 and y == 1:
+                for k in (2, 0, 1):
+                    arrived(y_in.at[k], y_recv.at[k])
+                    value = value + decode(y_in.at[k])
             for w in ways:
                 arrived(z_in.at[w, abs(zoff), y], z_recv.at[w, abs(zoff), y])
                 value = value + decode(z_in.at[w, abs(zoff), y])
             if zoff == 0 and y == 1:
-                for k in range(3):
-                    arrived(y_in.at[k], y_recv.at[k])
-                    value = value + decode(y_in.at[k])
                 grad_out[...] = value
                 continue
             out = z_out.at[i]

time: 70.3 us -> 69.9 us (level)
  no operation moved by 1% of the time
where the time goes in v5:
time: 69.9 us; the launch traced here: 69.8 us
  Pallas kernels  69.2 us (99%)
    pallas_call x1, Pallas kernels, body(): pl.pallas_call(functools.partial(kernel, blocks, reps, node_total), out_s...  67.4 us
    pallas_call x1, Pallas kernels, body(): pl.pallas_call(finish, out_shape=shapes, name='outputs')(act, grad_t, wgrad)  1.74 us

profile of v5, /device:TPU:1, one launch (start us, length us, event | category | flops | bytes accessed | tf_op | source)
XLA Modules:
  0.0 69.8 jit_solution(9076364339173785283)
XLA Ops:
  0.6 67.4 %graph_layer.1 = (f32[256,128]{1,0:T(8,128)}, f32[256,128]{1,0:T(8,128)}, f32[128,128]{1,0:T(8,128)}) custom-call(bf16[256,128]{1,0:T(8,128)(2,1)} %features.1, bf16[256,128,128]{2,1,0:T(8,128)(2,1)} %bitcast.9, s32[32]{0:T(128)} %bitcast.12, s32[8,32]{1,0:T(8,128)} %bitcast.10, s32[8,32]{1,0:T(8,128)} %bitcast.11, f32[128,128]{1,0:T(8,128)} %weight_hbm.1, ...), custom_call_target="tpu_custom_call" | custom-call | flops 2147483648 | bytes 8388608 | tf_op jit(solution)/shard_map/graph_layer/pallas_call | solution.py:454
  68.1 1.7 %outputs.1 = (f32[256,128]{1,0:T(8,128)}, f32[256,128]{1,0:T(8,128)}, f32[128,128]{1,0:T(8,128)}) custom-call(f32[256,128]{1,0:T(8,128)} %get-tuple-element.6.act, f32[256,128]{1,0:T(8,128)} %get-tuple-element.7.grad_t, f32[128,128]{1,0:T(8,128)} %get-tuple-element.8.wgrad), custom_call_target="tpu_custom_call" | custom-call | tf_op jit(solution)/shard_map/outputs/pallas_call | solution.py:508
